TPU v7x, 32 devices: a whole 2x2x4 slice. The times are simulated.
32 devices in a mesh: groups: 2 (over x), blk: 16 (over z, y, core).
Axes of the slice: x: 2, y: 2, z: 4, core: 2. Of those that a mesh axis runs over, the one named last changes fastest.
Arguments:
- train_acts: bfloat16 [4096, 768], P(('groups', 'blk')), parts along dimension 0, may hold values from -6 to 6
- train_grads: bfloat16 [4096, 2048], P(('groups', 'blk')), parts along dimension 0, may hold values from -0.059814453 to 0.059814453
- train_expert: int32 [4096, 1], P(('groups', 'blk')), parts along dimension 0, may hold values from 0 to 1; in each aligned block of 128 rows (0 to 127, 128 to 255, ...) at most 96 rows name the same one
- train_doc: int32 [4096], P(('groups', 'blk')), parts along dimension 0, may hold values from 0 to 3
- query_acts: bfloat16 [64, 768], P('blk'), may hold values from -6 to 6
- query_grads: bfloat16 [64, 2048], P('blk'), may hold values from -0.059814453 to 0.059814453
- query_expert: int32 [64, 1], P('blk'), may hold values from 0 to 1; in each aligned block of 4 rows (0 to 3, 4 to 7, ...) at most 3 rows name the same one
- query_ids: int32 [64], P('blk'), may hold values from 0 to 1
- basis_out: bfloat16 [2, 2048, 2048], P(None, None, 'blk'), may hold values from -0.125 to 0.125
- basis_in: bfloat16 [2, 768, 768], P(None, None, 'blk'), may hold values from -0.21875 to 0.21875
- eigenvalues: bfloat16 [2, 2048, 768], P(None, 'blk'), may hold values from 0.019897461 to 5
Outputs:
- scores: float32 [128, 32], P(('groups', 'blk')), parts along dimension 0
There are 2 independent parts, one for each index of `groups`. A program takes and returns all parts, laid end to end along the dimension named above; an argument that names none is the same for every part. Nothing has to cross between parts.
Inputs may be any that keep to these rules, and one draw needn't show every extreme that they name: `train_expert`: the rows of one device name each expert at most 96 times; in every draw some device's rows name one expert exactly 96 times. `query_expert`: the rows of one device name each expert at most 3 times; in every draw some device's rows name one expert exactly 3 times.
All inputs are finite; a program needn't handle non-finite values.
Results may differ from a plain program's by a relative error of at most 0.0053.
Values may be sent and summed in bfloat16 or wider, within the bound.
A program may use at most 128 MiB of HBM per device.

v0:
```python
import jax
import jax.numpy as jnp
from jax import lax
from jax.sharding import PartitionSpec as P

DOCS_DEV = 4
QRY_DEV = 2
CAP = 96
QCAP = 3


DAMPING = 0.05


def slot_table(experts, capacity, count):
    rows = experts.shape[0]
    onehot = (experts[:, None] == jnp.arange(count, dtype=jnp.int32)[None, :]).astype(jnp.int32)
    before = jnp.cumsum(onehot, axis=0) - onehot
    rank = jnp.sum(before * onehot, axis=1)
    target = experts * capacity + rank
    source = (
        jnp.zeros((count * capacity,), jnp.int32).at[target].set(jnp.arange(rows, dtype=jnp.int32))
    )
    filled = jnp.zeros((count * capacity,), jnp.int32).at[target].set(1)
    return (source.reshape(count, capacity), filled.reshape(count, capacity))


def turner(rows, piece):
    return jnp.einsum("ecd,edn->ecn", rows, piece, preferred_element_type=jnp.float32)


def body(
    train_acts,
    train_grads,
    train_expert,
    train_doc,
    query_acts,
    query_grads,
    query_expert,
    query_ids,
    basis_out,
    basis_in,
    eigenvalues,
):
    count = basis_out.shape[0]
    train_src, train_fill = slot_table(train_expert[:, 0], CAP, count)
    query_src, query_fill = slot_table(query_expert[:, 0], QCAP, count)
    source = jnp.concatenate([train_src, query_src + train_acts.shape[0]], axis=1)
    filled = jnp.concatenate([train_fill, query_fill], axis=1)
    weight = filled.astype(jnp.bfloat16)[:, :, None]
    grads_in = jnp.concatenate([train_grads, query_grads], axis=0)[source] * weight
    acts_in = jnp.concatenate([train_acts, query_acts], axis=0)[source] * weight
    slot_doc = train_doc[train_src]
    queries_total = QRY_DEV * lax.axis_size("blk")
    global_ids = jnp.where(
        query_fill == 1, lax.axis_index("blk") * QRY_DEV + query_ids[query_src], -1
    )
    rot_grads = turner(grads_in, lax.all_gather(basis_out, "blk", axis=2, tiled=True))
    rot_acts = turner(acts_in, lax.all_gather(basis_in, "blk", axis=2, tiled=True))
    rot_grads = rot_grads.astype(jnp.bfloat16)
    rot_acts = rot_acts.astype(jnp.bfloat16)
    train_g = rot_grads[:, :CAP]
    train_a = rot_acts[:, :CAP]
    query_g = rot_grads[:, CAP:]
    query_a = rot_acts[:, CAP:]
    doc_masks = [
        ((slot_doc == doc) & (train_fill == 1)).astype(jnp.bfloat16) for doc in range(DOCS_DEV)
    ]
    scale = lax.all_gather(eigenvalues, "blk", axis=1, tiled=True).astype(jnp.float32) + DAMPING
    mats = []
    for mask in doc_masks:
        summed = jnp.einsum(
            "ecn,ecf->enf", train_g * mask[:, :, None], train_a, preferred_element_type=jnp.float32
        )
        mats.append((summed / scale).astype(jnp.bfloat16))
    doc_mats = jnp.stack(mats)
    piece_g, piece_a, piece_ids = lax.all_gather(
        (query_g, query_a, global_ids), "blk", axis=1, tiled=True
    )
    image = jnp.einsum("esf,kedf->kesd", piece_a, doc_mats, preferred_element_type=jnp.float32)
    token = jnp.einsum("kesd,esd->esk", image, piece_g.astype(jnp.float32))
    table = (
        piece_ids.reshape(-1)[:, None] == jnp.arange(queries_total, dtype=jnp.int32)[None, :]
    ).astype(jnp.float32)
    return jnp.dot(token.reshape(-1, DOCS_DEV).T, table, precision=lax.Precision.HIGHEST)


def solution(mesh):
    in_specs = (
        P(("groups", "blk"), None),
        P(("groups", "blk"), None),
        P(("groups", "blk"), None),
        P(("groups", "blk")),
        P("blk", None),
        P("blk", None),
        P("blk", None),
        P("blk"),
        P(None, None, "blk"),
        P(None, None, "blk"),
        P(None, "blk", None),
    )
    out_specs = P(("groups", "blk"), None)
    return jax.shard_map(body, mesh=mesh, in_specs=in_specs, out_specs=out_specs, check_vma=False)
```

profile of v0, /device:TPU:0, one launch (start us, length us, event | category | flops | bytes accessed | tf_op | source)
XLA Modules:
  0.0 286.9 jit_solution(85553088531195338)
XLA Ops:
  6.5 0.0 copy-start
  6.5 0.0 all-gather.7.cloned.1.call-start
  6.5 0.7 all-gather.7.cloned.1.call-update
  7.3 0.0 all-gather.5.cloned.1.call-start
  7.3 0.7 all-gather.5.cloned.1.call-update
  8.0 0.0 copy-start.1
  8.0 0.0 copy-start.2
  8.0 0.0 all-gather.9.cloned.1.call-start
  8.1 0.7 all-gather.9.cloned.1.call-update
  8.8 0.7 fusion.36
  9.4 0.2 reduce_window_sum.23
  9.6 0.7 select_reduce_fusion.1
  10.3 0.7 fusion.38
  10.9 0.6 scatter_custom_fusion.1
  11.5 0.1 reshape.201
  11.6 0.1 reshape.234
  11.7 0.6 scatter_custom_fusion.3
  12.3 1.3 gather_fusion.3
  13.6 0.1 reshape.203
  13.7 0.7 fusion.33
  14.5 0.2 reduce_window_sum.22
  14.6 0.8 select_reduce_fusion
  15.5 0.7 fusion.37
  16.1 1.0 scatter_custom_fusion.2
  17.1 0.1 reshape.202
  17.2 1.0 scatter_custom_fusion
  18.2 0.1 concatenate.45
  18.3 0.1 concatenate.46
  18.4 0.1 compare_select_fusion.2
  18.4 0.1 reshape.210
  18.5 1.1 pad_maximum_fusion.1
  19.7 1.2 gather_fusion
  20.8 0.2 reshape.209
  21.0 0.0 copy-done.1
  21.0 0.0 copy-done.2
  21.1 1.0 gather_fusion.2
  22.1 0.1 reshape.225
  22.2 0.1 reshape.218
  22.3 0.0 copy-done
  22.3 1.6 gather_fusion.1
  23.9 0.1 reshape.293
  24.0 0.1 reshape.294
  24.0 0.1 reshape.295
  24.1 0.1 reshape.292
  24.2 0.1 reshape.291
  24.3 23.1 %all-gather = s32[16,3,2]{1,2,0:T(2,128)S(1)} all-gather(s32[1,3,2]{1,2,0:T(2,128)S(1)} %bitcast.49), channel_id=1, replica_groups=mesh['groups'=2,'blk'=16] {'blk'}, dimensions={0}, use_global_device_ids=true | all-gather | bytes 408 | tf_op jit(solution)/shard_map/all_gather | solution.py:77
  47.4 0.1 reshape.297
  47.5 0.1 eq.117
  47.6 0.1 pad_maximum_fusion.3
  47.6 7.1 %all-gather.7.cloned.1.call-done = bf16[2,768,768]{1,2,0:T(8,128)(2,1)} async-done(((bf16[2,768,48]{1,2,0:T(8,128)(2,1)}), bf16[2,768,768]{1,2,0:T(8,128)(2,1)}) %all-gather.7.cloned.1.call-update) | async-done | bytes 2359312 | tf_op jit(solution)/shard_map/all_gather | solution.py:59
  54.8 2.5 convolution_convert_fusion.1
  57.3 20.2 %all_gather.21 = bf16[2,48,768]{2,0,1:T(2,128)(2,1)S(1)} all-gather(bf16[2,3,768]{2,0,1:T(2,128)(2,1)S(1)} %copy.20), channel_id=1, replica_groups=mesh['groups'=2,'blk'=16] {'blk'}, dimensions={1}, use_global_device_ids=true | all-gather | bytes 156672 | tf_op jit(solution)/shard_map/all_gather | solution.py:77
  77.5 109.2 %all-gather.5.cloned.1.call-done = bf16[2,2048,2048]{2,1,0:T(8,128)(2,1)} async-done(((bf16[2,2048,128]{2,1,0:T(8,128)(2,1)}), bf16[2,2048,2048]{2,1,0:T(8,128)(2,1)}) %all-gather.5.cloned.1.call-update) | async-done | bytes 16777232 | tf_op jit(solution)/shard_map/all_gather | solution.py:58
  186.7 8.5 %convolution_convert_fusion = bf16[2,99,2048]{2,1,0:T(8,128)(2,1)S(1)} fusion(bf16[2,2048,2048]{2,1,0:T(8,128)(2,1)} %all-gather.5.cloned.1.call-done, bf16[2,99,2048]{2,1,0:T(8,128)(2,1)S(1)} %reshape.209, bf16[2,99]{1,0:T(2,128)(2,1)S(1)} %pad_maximum_fusion.3), kind=kOutput, calls=%fused_computation.23 | convolution fusion | flops 1661755392 | bytes 18399628 | tf_op jit(solution)/shard_map/ecd,edn->ecn/dot_general | solution.py:29
  195.2 22.0 %all_gather.22 = bf16[2,48,2048]{2,0,1:T(2,128)(2,1)S(1)} all-gather(bf16[2,3,2048]{2,0,1:T(2,128)(2,1)S(1)} %copy.23), channel_id=1, replica_groups=mesh['groups'=2,'blk'=16] {'blk'}, dimensions={1}, use_global_device_ids=true | all-gather | bytes 417792 | tf_op jit(solution)/shard_map/all_gather | solution.py:77
  217.2 33.7 %all-gather.9.cloned.1.call-done = bf16[2,2048,768]{2,1,0:T(8,128)(2,1)} async-done(((bf16[2,128,768]{2,1,0:T(8,128)(2,1)}), bf16[2,2048,768]{2,1,0:T(8,128)(2,1)}) %all-gather.9.cloned.1.call-update) | async-done | bytes 6291472 | tf_op jit(solution)/shard_map/all_gather | solution.py:69
  250.9 4.9 %fusion.3 = bf16[1,2,2048,768]{3,2,1,0:T(8,128)(2,1)S(1)} fusion(bf16[2,2048,768]{2,1,0:T(8,128)(2,1)} %all-gather.9.cloned.1.call-done, bf16[2,99,2048]{2,1,0:T(8,128)(2,1)S(1)} %convolution_convert_fusion, bf16[2,96]{1,0:T(2,128)(2,1)S(1)} %reshape.293, bf16[2,99,768]{2,1,0:T(8,128)(2,1)S(1)} %convolution_convert_fusion.1), kind=kOutput, calls=%fused_computation.17 | convolution fusion | flops 616955904 | bytes 13664768 | tf_op jit(solution)/shard_map/ecn,ecf->enf/dot_general | solution.py:72
  255.7 0.0 copy-done.3
  255.8 2.5 fusion.4
  258.3 4.2 %fusion.5 = bf16[1,2,2048,768]{3,2,1,0:T(8,128)(2,1)} fusion(bf16[2,2048,768]{2,1,0:T(8,128)(2,1)S(1)} %copy-done.3, bf16[2,99,2048]{2,1,0:T(8,128)(2,1)S(1)} %convolution_convert_fusion, bf16[2,96]{1,0:T(2,128)(2,1)S(1)} %reshape.295, bf16[2,99,768]{2,1,0:T(8,128)(2,1)S(1)} %convolution_convert_fusion.1), kind=kOutput, calls=%fused_computation.19 | convolution fusion | flops 616955904 | bytes 13664768 | tf_op jit(solution)/shard_map/ecn,ecf->enf/dot_general | solution.py:72
  262.4 4.1 %fusion.2 = bf16[1,2,2048,768]{3,2,1,0:T(8,128)(2,1)} fusion(bf16[2,2048,768]{2,1,0:T(8,128)(2,1)S(1)} %copy-done.3, bf16[2,99,2048]{2,1,0:T(8,128)(2,1)S(1)} %convolution_convert_fusion, bf16[2,96]{1,0:T(2,128)(2,1)S(1)} %reshape.292, bf16[2,99,768]{2,1,0:T(8,128)(2,1)S(1)} %convolution_convert_fusion.1), kind=kOutput, calls=%fused_computation.16 | convolution fusion | flops 616955904 | bytes 13664768 | tf_op jit(solution)/shard_map/ecn,ecf->enf/dot_general | solution.py:72
  266.5 10.9 %fusion.8 = bf16[4,2,48,2048]{3,2,0,1:T(8,128)(2,1)S(1)} fusion(bf16[2,48,768,1]{2,0,1,3:T(2,128)(2,1)S(1)} %bitcast.46, bf16[1,2,2048,768]{3,2,1,0:T(8,128)(2,1)} %fusion.5, bf16[1,2,2048,768]{3,2,1,0:T(8,128)(2,1)S(1)} %fusion.4, bf16[1,2,2048,768]{3,2,1,0:T(8,128)(2,1)S(1)} %fusion.3, bf16[1,2,2048,768]{3,2,1,0:T(8,128)(2,1)} %fusion.2), kind=kOutput, calls=%fused_computation.22 | convolution fusion | flops 1245708288 | bytes 26886144 | tf_op jit(solution)/shard_map/esf,kedf->kesd/dot_general | solution.py:80
  277.4 2.2 fusion.6
  279.6 0.8 fusion.34
  (21 shorter events, 0.2 us)
Async XLA Ops:
  6.5 15.7 %copy-start = (s32[128]{0:T(128)S(1)}, s32[128]{0:T(128)}, u32[]{:S(2)}) copy-start(s32[128]{0:T(128)} %param.14) | copy-start | bytes 1540
  6.5 48.2 %all-gather.7.cloned.1.call-start = ((), (), s32[]{:S(2)}) async-start(), calls=%async_computation.1 | async-start | bytes 2506752 | tf_op jit(solution)/shard_map/all_gather | solution.py:59
  7.3 179.4 %all-gather.5.cloned.1.call-start = ((), (), s32[]{:S(2)}) async-start(), calls=%async_computation | async-start | bytes 17825792 | tf_op jit(solution)/shard_map/all_gather | solution.py:58
  8.0 13.0 %copy-start.1 = (bf16[128,768]{1,0:T(8,128)(2,1)S(1)}, bf16[128,768]{1,0:T(8,128)(2,1)}, u32[]{:S(2)}) copy-start(bf16[128,768]{1,0:T(8,128)(2,1)} %param.11) | copy-start | bytes 589828
  8.0 13.0 %copy-start.2 = (bf16[4,768]{1,0:T(4,128)(2,1)S(1)}, bf16[4,768]{1,0:T(4,128)(2,1)}, u32[]{:S(2)}) copy-start(bf16[4,768]{1,0:T(4,128)(2,1)} %param.15) | copy-start | bytes 18436
  8.0 242.9 %all-gather.9.cloned.1.call-start = ((), (), s32[]{:S(2)}) async-start(), calls=%async_computation.2 | async-start | bytes 6684672 | tf_op jit(solution)/shard_map/all_gather | solution.py:69
  250.9 4.9 %copy-start.3 = (bf16[2,2048,768]{2,1,0:T(8,128)(2,1)S(1)}, bf16[2,2048,768]{2,1,0:T(8,128)(2,1)}, u32[]{:S(2)}) copy-start(bf16[2,2048,768]{2,1,0:T(8,128)(2,1)} %all-gather.9.cloned.1.call-done) | copy-start | bytes 18874372
Sparse Core Ops, SparseCore 0:
  9.6 45.0 all-gather.6
  56.9 129.7 all-gather.4
  189.0 61.8 all-gather.8
where the time goes:
time: 287 us
  waiting for transfers between devices  152 us (53%)
  blocking collectives  65.3 us (23%)
  matrix products  40.5 us (14%)
  between operations  13.4 us (5%)
  local copies, waits for them, and re-layouts  9.76 us (3%)
  other arithmetic  5.92 us (2%)
    all_gather x1, waiting for transfers between devices, body(): lax.all_gather(basis_out, 'blk', axis=2, tiled=True)  109 us
    all_gather x3, blocking collectives, body(): lax.all_gather((query_g, query_a, global_ids), 'blk', axis=1, tiled=True)  65.3 us
    all_gather x1, waiting for transfers between devices, body(): lax.all_gather(eigenvalues, 'blk', axis=1, tiled=True).astype(jnp.float32)  33.7 us
    dot_general x4, matrix products, body(): jnp.einsum('ecn,ecf->enf', train_g * mask[:, :, None], train_a, preferred...  15.6 us
    dot_general x2, matrix products, turner(): jnp.einsum('ecd,edn->ecn', rows, piece, preferred_element_type=jnp.float32)  11 us
    dot_general x1, matrix products, body(): jnp.einsum('esf,kedf->kesd', piece_a, doc_mats, preferred_element_type=jn...  10.9 us
    all_gather x1, waiting for transfers between devices, body(): lax.all_gather(basis_in, 'blk', axis=2, tiled=True)  7.12 us
  transfers between devices with their start and end apart: 3, of which 3 were waited for; matrix products, arithmetic and copies ran while one was open for 9% of the time, Pallas kernels for 0%

commit v1 on v0

--- a/solution.py
+++ b/solution.py
@@ -1,22 +1,289 @@
 import jax
 import jax.numpy as jnp
 from jax import lax
+from jax.experimental import pallas as pl
+from jax.experimental.pallas import tpu as pltpu
 from jax.sharding import PartitionSpec as P
 
 DOCS_DEV = 4
 QRY_DEV = 2
 CAP = 96
 QCAP = 3
-
-
 DAMPING = 0.05
+LANES = 128
+COPIES = 25
+LOCALS = 5
+MESH = pl.DeviceIdType.MESH
+
+
+def kernel(
+    grads_in, acts_in, bo_in, ei_in, pk_in, out_ref,
+    rows, acts, bo, ei, biq, bit, rot_a, qn, qat, qgt, rc, gt, tok, got,
+    send, recv, local,
+):
+    x = lax.axis_index("groups")
+    b = lax.axis_index("blk")
+    c, y, z = b % 2, (b // 2) % 2, b // 4
+    z1 = z + 1 - 2 * (z % 2)
+    z2 = (z + 2) % 4
+
+    def at(xx, zz, yy, cc):
+        return (xx, (zz * 2 + yy) * 2 + cc)
+
+    to_z1, to_z2 = at(x, z1, y, c), at(x, z2, y, c)
+    to_y, to_x = at(x, z, 1 - y, c), at(1 - x, z, y, c)
+    to_c, to_d = at(x, z, y, 1 - c), at(x, z1, 1 - y, c)
+    barrier = pltpu.get_barrier_semaphore()
+    for peer in (to_z1, to_z2, to_y, to_x, to_c, to_d):
+        pl.semaphore_signal(barrier, inc=1, device_id=peer, device_id_type=MESH)
+
+    def put(i, src, dst, peer):
+        return pltpu.make_async_remote_copy(
+            src_ref=src, dst_ref=dst, send_sem=send.at[i], recv_sem=recv.at[i],
+            device_id=peer, device_id_type=MESH,
+        )
+
+    T = LANES
+    ox = 1 - x
+    cp = [
+        put(0, grads_in, rows.at[pl.ds(T, T)], to_z1),
+        put(1, acts_in, acts.at[pl.ds(T, T)], to_z1),
+        put(2, grads_in, rows.at[pl.ds(2 * T, T)], to_y),
+        put(3, acts_in, acts.at[pl.ds(2 * T, T)], to_y),
+        put(4, rows.at[pl.ds(T, T)], rows.at[pl.ds(3 * T, T)], to_y),
+        put(5, acts.at[pl.ds(T, T)], acts.at[pl.ds(3 * T, T)], to_y),
+        put(6, bo_in.at[x], bo.at[1, x], to_z2),
+        put(7, ei_in.at[x], ei.at[1, x], to_z2),
+        put(8, bo.at[1, x], bo.at[1, x], to_x),
+        put(9, ei.at[1, x], ei.at[1, x], to_x),
+        put(10, bo_in, bo.at[2], to_c),
+        put(11, ei_in, ei.at[2], to_c),
+        put(12, bo.at[1, x], bo.at[3, x], to_c),
+        put(13, ei.at[1, x], ei.at[3, x], to_c),
+        put(14, bo.at[1, ox], bo.at[3, ox], to_c),
+        put(15, ei.at[1, ox], ei.at[3, ox], to_c),
+        put(16, pk_in.at[x], biq.at[x, 1], to_z2),
+        put(17, biq.at[x, pl.ds(0, 2)], biq.at[x, pl.ds(2, 2)], to_z1),
+        put(18, biq.at[x, pl.ds(0, 4)], biq.at[x, pl.ds(4, 4)], to_y),
+        put(19, biq.at[x, pl.ds(0, 8)], biq.at[x, pl.ds(0, 8)], to_x),
+        put(20, biq.at[x, pl.ds(0, 8)], biq.at[x, pl.ds(8, 8)], to_c),
+        put(21, biq.at[ox, pl.ds(0, 8)], biq.at[ox, pl.ds(8, 8)], to_c),
+        put(22, tok.at[1], got.at[0], to_z1),
+        put(23, tok.at[2], got.at[1], to_y),
+        put(24, tok.at[3], got.at[2], to_d),
+    ]
+    here = [
+        pltpu.make_async_copy(pk_in.at[x], biq.at[x, 0], local.at[0]),
+        pltpu.make_async_copy(grads_in, rows.at[pl.ds(0, T)], local.at[1]),
+        pltpu.make_async_copy(acts_in, acts.at[pl.ds(0, T)], local.at[2]),
+        pltpu.make_async_copy(bo_in, bo.at[0], local.at[3]),
+        pltpu.make_async_copy(ei_in, ei.at[0], local.at[4]),
+    ]
+    for one in here:
+        one.start()
+    pl.semaphore_wait(barrier, 6)
+
+    def go(*which):
+        for i in which:
+            cp[i].start()
+
+    def came(*which):
+        for i in which:
+            cp[i].wait_recv()
+
+    go(16, 1, 0, 6, 7, 3, 2, 11, 10)
+    here[0].wait()
+    came(16)
+    go(17)
+    came(17)
+    go(18)
+    came(1, 0)
+    go(5, 4)
+    came(18)
+    go(20, 19)
+    for one in here[1:]:
+        one.wait()
+
+    def recips(j):
+        for e in range(2):
+            def step(i, _):
+                at_rows = pl.ds(pl.multiple_of(i * 16, 16), 16)
+                rc[e, j, at_rows, :] = 1.0 / (ei[j, e, at_rows, :].astype(jnp.float32) + DAMPING)
+                return 0
+            lax.fori_loop(0, 8, step, 0)
+
+    recips(0)
+    came(11, 10)
+    recips(2)
+    came(6, 7)
+    go(9, 8, 13, 12)
+    came(19)
+    go(21)
+    came(20, 21)
+
+    for other in range(16):
+        oc, oy, oz = other % 2, (other // 2) % 2, other // 4
+        slot = (
+            jnp.where(z // 2 != oz // 2, 1, 0)
+            + jnp.where(z % 2 != oz % 2, 2, 0)
+            + jnp.where(y != oy, 4, 0)
+            + jnp.where(c != oc, 8, 0)
+        )
+        for e in range(2):
+            bit[e, 48 * other : 48 * other + 48, :] = biq[e, slot, 0:48, :]
+        qn[16 * other : 16 * other + 16, :] = biq[0, slot, 48:64, :]
+
+    s_at = lax.broadcasted_iota(jnp.int32, (T, 2 * T), 0)
+    r_at = lax.broadcasted_iota(jnp.int32, (T, 2 * T), 1)
+    quarter = []
+    for j in range(4):
+        pick = jnp.where(r_at == 4 * s_at + j, 1.0, 0.0).astype(jnp.bfloat16)
+        quarter.append(
+            jnp.dot(pick, qn[...], preferred_element_type=jnp.float32).astype(jnp.bfloat16)
+        )
+    Q = 4 * T
+    rows[Q : Q + T, 0:768] = quarter[0]
+    rows[Q : Q + T, 768:1536] = quarter[1]
+    rows[Q : Q + T, 1536:2048] = quarter[2][:, 0:512]
+    acts[Q : Q + T, 0:256] = quarter[2][:, 512:768]
+    acts[Q : Q + T, 256:896] = quarter[3][:, 0:640]
+    ident = quarter[3][:, 640:768].astype(jnp.float32)
+
+    def code_of(slot):
+        at_rows = pl.ds(pl.multiple_of(slot * T, T), T)
+        return at_rows, acts[at_rows, 768:896].astype(jnp.float32)
+
+    came(3, 2, 5, 4)
+
+    def turn_acts(slot, _):
+        at_rows, code = code_of(slot)
+        second = jnp.concatenate([code] * 6, axis=1) >= 4.0
+        each = [
+            lax.dot_general(
+                acts[at_rows, 0:768], bit[e], (((1,), (1,)), ((), ())),
+                preferred_element_type=jnp.float32,
+            )
+            for e in range(2)
+        ]
+        rot_a[at_rows, :] = jnp.where(second, each[1], each[0]).astype(jnp.bfloat16)
+        return 0
+
+    lax.fori_loop(0, 5, turn_acts, 0)
+    _, qcode = code_of(4)
+    qsecond = jnp.concatenate([qcode] * 6, axis=1) >= 4.0
+    turned = rot_a[Q : Q + T, :].astype(jnp.float32)
+    qat[0] = jnp.where(qsecond, 0.0, turned).T.astype(jnp.bfloat16)
+    qat[1] = jnp.where(qsecond, turned, 0.0).T.astype(jnp.bfloat16)
+    tok[...] = jnp.zeros_like(tok)
+
+    def columns(first, last):
+        def turn_grads(slot, _):
+            at_rows, code = code_of(slot)
+            second = jnp.concatenate([code] * 2, axis=1) >= 4.0
+            each = [
+                jnp.dot(
+                    rows[at_rows, :],
+                    jnp.concatenate([bo[first, e], bo[last, e]], axis=1),
+                    preferred_element_type=jnp.float32,
+                )
+                for e in range(2)
+            ]
+            gt[slot] = jnp.where(second, each[1], each[0]).T.astype(jnp.bfloat16)
+            return 0
+
+        lax.fori_loop(0, 5, turn_grads, 0)
+        qgt[...] = gt[4].astype(jnp.float32)
+
+        def score(slot, _):
+            at_rows, code = code_of(slot)
+            wide = jnp.concatenate([code] * 6, axis=1)
+            ra = rot_a[at_rows, :].astype(jnp.float32)
+            for doc in range(DOCS_DEV):
+                image = jnp.zeros((2 * T, T), jnp.float32)
+                for e in range(2):
+                    kept = jnp.where(wide == float(4 * e + doc), ra, 0.0).astype(jnp.bfloat16)
+                    summed = jnp.dot(gt[slot], kept, preferred_element_type=jnp.float32)
+                    scale = jnp.concatenate([rc[e, first], rc[e, last]], axis=0)
+                    mat = (summed * scale).astype(jnp.bfloat16)
+                    image = image + jnp.dot(mat, qat[e], preferred_element_type=jnp.float32)
+                part = jnp.sum(image * qgt[...], axis=0, keepdims=True)
+                tok[slot, doc : doc + 1, :] = tok[slot, doc : doc + 1, :] + part
+            return 0
+
+        lax.fori_loop(0, 4, score, 0)
+
+    columns(0, 2)
+    came(9, 8)
+    go(15, 14)
+    recips(1)
+    came(13, 12, 15, 14)
+    recips(3)
+    columns(1, 3)
+
+    go(22, 23, 24)
+    s_f = lax.broadcasted_iota(jnp.int32, (T, T), 0)
+    q_f = lax.broadcasted_iota(jnp.int32, (T, T), 1).astype(jnp.float32)
+    owner = ((s_f // 4) * QRY_DEV).astype(jnp.float32)
+    table = jnp.where(owner + ident == q_f, 1.0, 0.0)
+    came(22, 23, 24)
+    total = tok[0] + got[0] + got[1] + got[2]
+    res = jnp.dot(
+        total, table, precision=lax.Precision.HIGHEST, preferred_element_type=jnp.float32
+    )
+    out_ref[...] = res[0:4, 0:32]
+    for one in cp:
+        one.wait_send()
+
+
+def fused(
+    train_acts, train_grads, train_expert, train_doc, query_acts, query_grads,
+    query_expert, query_ids, basis_out, basis_in, eigenvalues,
+):
+    bf = jnp.bfloat16
+    code = (train_expert * 4 + train_doc[:, None]).astype(bf)
+    acts_in = jnp.concatenate([train_acts, jnp.broadcast_to(code, (LANES, LANES))], axis=1)
+    qcode = jnp.broadcast_to((query_expert * 4).astype(bf), (4, LANES))
+    qident = jnp.broadcast_to(query_ids.astype(bf)[:, None], (4, LANES))
+    qpack = jnp.concatenate([query_grads, query_acts, qcode, qident], axis=1).reshape(1, 16, 768)
+    qpack = jnp.concatenate([qpack, jnp.zeros_like(qpack)], axis=0)
+    pk_in = jnp.concatenate([jnp.swapaxes(basis_in, 1, 2), qpack], axis=1)
+    anywhere = pl.BlockSpec(memory_space=pl.ANY)
+    f32 = jnp.float32
+    return pl.pallas_call(
+        kernel,
+        out_shape=jax.ShapeDtypeStruct((4, 32), f32),
+        in_specs=[anywhere] * 5,
+        out_specs=pl.BlockSpec(memory_space=pltpu.VMEM),
+        scratch_shapes=[
+            pltpu.VMEM((5 * LANES, 2048), bf),
+            pltpu.VMEM((5 * LANES, 896), bf),
+            pltpu.VMEM((4, 2, 2048, LANES), bf),
+            pltpu.VMEM((4, 2, LANES, 768), bf),
+            pltpu.VMEM((2, 16, 64, 768), bf),
+            pltpu.VMEM((2, 768, 768), bf),
+            pltpu.VMEM((5 * LANES, 768), bf),
+            pltpu.VMEM((2 * LANES, 768), bf),
+            pltpu.VMEM((2, 768, LANES), bf),
+            pltpu.VMEM((2 * LANES, LANES), f32),
+            pltpu.VMEM((2, 4, LANES, 768), f32),
+            pltpu.VMEM((5, 2 * LANES, LANES), bf),
+            pltpu.VMEM((4, 8, LANES), f32),
+            pltpu.VMEM((3, 8, LANES), f32),
+            pltpu.SemaphoreType.DMA((COPIES,)),
+            pltpu.SemaphoreType.DMA((COPIES,)),
+            pltpu.SemaphoreType.DMA((LOCALS,)),
+        ],
+        compiler_params=pltpu.CompilerParams(
+            collective_id=0, has_side_effects=True, vmem_limit_bytes=48 * 2**20
+        ),
+    )(train_grads, acts_in, basis_out, eigenvalues, pk_in)
 
 
 def slot_table(experts, capacity, count):
     rows = experts.shape[0]
-    onehot = (experts[:, None] == jnp.arange(count, dtype=jnp.int32)[None, :]).astype(jnp.int32)
-    before = jnp.cumsum(onehot, axis=0) - onehot
-    rank = jnp.sum(before * onehot, axis=1)
+    place = jnp.arange(rows, dtype=jnp.int32)
+    ahead = (experts[:, None] == experts[None, :]) & (place[None, :] < place[:, None])
+    rank = jnp.sum(ahead.astype(jnp.int32), axis=1)
     target = experts * capacity + rank
     source = (
         jnp.zeros((count * capacity,), jnp.int32).at[target].set(jnp.arange(rows, dtype=jnp.int32))
@@ -100,4 +367,6 @@
         P(None, "blk", None),
     )
     out_specs = P(("groups", "blk"), None)
-    return jax.shard_map(body, mesh=mesh, in_specs=in_specs, out_specs=out_specs, check_vma=False)
+    sizes = (mesh.shape["groups"], mesh.shape["blk"])
+    chosen = fused if sizes == (2, 16) else body
+    return jax.shard_map(chosen, mesh=mesh, in_specs=in_specs, out_specs=out_specs, check_vma=False)

time: 287 us -> 115 us (0.40)
  waiting for transfers between devices: 152 us -> 0 us
  Pallas kernels: 0 us -> 108 us
  blocking collectives: 65.3 us -> 0 us
  matrix products: 40.5 us -> 0 us
  between operations: 13.4 us -> 0.07 us
  local copies, waits for them, and re-layouts: 9.76 us -> 2.06 us
    all_gather x3 -> x0, waiting for transfers between devices: 150 us -> none  [the longest x1 109 us: body(): lax.all_gather(basis_out, 'blk', axis=2, tiled=True)]
    pallas_call x0 -> x1, Pallas kernels: none -> 108 us  [fused(): pl.pallas_call(kernel, out_shape=jax.ShapeDtypeStruct((4, 32), f32), in_s...]
    all_gather x3 -> x0, blocking collectives: 65.3 us -> none  [body(): lax.all_gather((query_g, query_a, global_ids), 'blk', axis=1, tiled=True)]
    dot_general x9 -> x0, matrix products: 40.5 us -> none  [the longest x4 15.6 us: body(): jnp.einsum('ecn,ecf->enf', train_g * mask[:, :, None], train_a, preferred...]
    gather x6 -> x0, local copies, waits for them, and re-layouts: 5.29 us -> none  [the longest x1 1.55 us: body(): slot_doc = train_doc[train_src]]
    scatter x4 -> x0, local copies, waits for them, and re-layouts: 3.11 us -> none  [the longest x2 1.56 us: slot_table(): jnp.zeros((count * capacity,), jnp.int32).at[target]]
  transfers between devices with their start and end apart: 3 -> 0, of which waited for: 3 -> 0; matrix products, arithmetic and copies ran while one was open for 9% -> 0% of each run, Pallas kernels for 0% -> 0%
where the time goes in v1:
time: 115 us
  Pallas kernels  108 us (94%)
  other arithmetic  4.73 us (4%)
  local copies, waits for them, and re-layouts  2.06 us (2%)
    pallas_call x1, Pallas kernels, fused(): pl.pallas_call(kernel, out_shape=jax.ShapeDtypeStruct((4, 32), f32), in_s...  108 us

profile of v1, /device:TPU:0, one launch (start us, length us, event | category | flops | bytes accessed | tf_op | source)
XLA Modules:
  0.0 114.9 jit_solution(1853864029877759213)
XLA Ops:
  0.0 0.0 copy-start.1
  0.0 0.7 fusion.3
  0.7 0.1 broadcast_in_dim.26
  0.8 0.0 copy-start.2
  0.8 1.0 pad_maximum_fusion.acts_in
  1.8 0.7 convert_bitcast_fusion
  2.5 0.1 broadcast_in_dim.28
  2.6 0.7 convert_element_type.11
  3.2 0.1 broadcast_in_dim.29
  3.3 0.7 pad_maximum_fusion.1
  4.1 0.9 fusion.1.pk_in
  5.0 0.0 copy-done.1
  5.0 0.0 copy-done.2
  5.0 0.0 copy-start
  5.1 1.2 %copy-done = bf16[2,2048,128]{2,1,0:T(8,128)(2,1)S(1)} copy-done((bf16[2,2048,128]{2,1,0:T(8,128)(2,1)S(1)}, bf16[2,2048,128]{2,1,0:T(8,128)(2,1)}, u32[]{:S(2)}) %copy-start) | copy-done | bytes 1048600
  6.3 108.0 %shard_map.109 = f32[4,32]{1,0:T(4,128)S(1)} custom-call(bf16[128,2048]{1,0:T(8,128)(2,1)S(1)} %copy-done.1, bf16[128,896]{1,0:T(8,128)(2,1)S(1)} %pad_maximum_fusion.acts_in, bf16[2,2048,128]{2,1,0:T(8,128)(2,1)S(1)} %copy-done, bf16[2,128,768]{2,1,0:T(8,128)(2,1)S(1)} %copy-done.2, bf16[2,64,768]{2,1,0:T(8,128)(2,1)S(1)} %fusion.1.pk_in), custom_call_target="tpu_custom_call" | custom-call | tf_op jit(solution)/shard_map/pallas_call | solution.py:252
  114.3 0.6 copy.13
  (1 shorter events, 0.0 us)
Async XLA Ops:
  0.0 5.0 %copy-start.1 = (bf16[128,2048]{1,0:T(8,128)(2,1)S(1)}, bf16[128,2048]{1,0:T(8,128)(2,1)}, u32[]{:S(2)}) copy-start(bf16[128,2048]{1,0:T(8,128)(2,1)} %grads_in.1) | copy-start | bytes 1572868
  0.8 4.2 %copy-start.2 = (bf16[2,128,768]{2,1,0:T(8,128)(2,1)S(1)}, bf16[2,128,768]{2,1,0:T(8,128)(2,1)}, u32[]{:S(2)}) copy-start(bf16[2,128,768]{2,1,0:T(8,128)(2,1)} %ei_in.1) | copy-start | bytes 1179652
  5.0 1.2 %copy-start = (bf16[2,2048,128]{2,1,0:T(8,128)(2,1)S(1)}, bf16[2,2048,128]{2,1,0:T(8,128)(2,1)}, u32[]{:S(2)}) copy-start(bf16[2,2048,128]{2,1,0:T(8,128)(2,1)} %bo_in.1) | copy-start | bytes 3145732

commit v2 on v1

--- a/solution.py
+++ b/solution.py
@@ -11,7 +11,8 @@
 QCAP = 3
 DAMPING = 0.05
 LANES = 128
-COPIES = 25
+COPIES = 40
+PARTS = 4
 LOCALS = 5
 MESH = pl.DeviceIdType.MESH
 
@@ -33,6 +34,7 @@
     to_z1, to_z2 = at(x, z1, y, c), at(x, z2, y, c)
     to_y, to_x = at(x, z, 1 - y, c), at(1 - x, z, y, c)
     to_c, to_d = at(x, z, y, 1 - c), at(x, z1, 1 - y, c)
+    used = []
     barrier = pltpu.get_barrier_semaphore()
     for peer in (to_z1, to_z2, to_y, to_x, to_c, to_d):
         pl.semaphore_signal(barrier, inc=1, device_id=peer, device_id_type=MESH)
@@ -45,33 +47,50 @@
 
     T = LANES
     ox = 1 - x
-    cp = [
-        put(0, grads_in, rows.at[pl.ds(T, T)], to_z1),
-        put(1, acts_in, acts.at[pl.ds(T, T)], to_z1),
-        put(2, grads_in, rows.at[pl.ds(2 * T, T)], to_y),
-        put(3, acts_in, acts.at[pl.ds(2 * T, T)], to_y),
-        put(4, rows.at[pl.ds(T, T)], rows.at[pl.ds(3 * T, T)], to_y),
-        put(5, acts.at[pl.ds(T, T)], acts.at[pl.ds(3 * T, T)], to_y),
-        put(6, bo_in.at[x], bo.at[1, x], to_z2),
-        put(7, ei_in.at[x], ei.at[1, x], to_z2),
-        put(8, bo.at[1, x], bo.at[1, x], to_x),
-        put(9, ei.at[1, x], ei.at[1, x], to_x),
-        put(10, bo_in, bo.at[2], to_c),
-        put(11, ei_in, ei.at[2], to_c),
-        put(12, bo.at[1, x], bo.at[3, x], to_c),
-        put(13, ei.at[1, x], ei.at[3, x], to_c),
-        put(14, bo.at[1, ox], bo.at[3, ox], to_c),
-        put(15, ei.at[1, ox], ei.at[3, ox], to_c),
-        put(16, pk_in.at[x], biq.at[x, 1], to_z2),
-        put(17, biq.at[x, pl.ds(0, 2)], biq.at[x, pl.ds(2, 2)], to_z1),
-        put(18, biq.at[x, pl.ds(0, 4)], biq.at[x, pl.ds(4, 4)], to_y),
-        put(19, biq.at[x, pl.ds(0, 8)], biq.at[x, pl.ds(0, 8)], to_x),
-        put(20, biq.at[x, pl.ds(0, 8)], biq.at[x, pl.ds(8, 8)], to_c),
-        put(21, biq.at[ox, pl.ds(0, 8)], biq.at[ox, pl.ds(8, 8)], to_c),
-        put(22, tok.at[1], got.at[0], to_z1),
-        put(23, tok.at[2], got.at[1], to_y),
-        put(24, tok.at[3], got.at[2], to_d),
+    R, K = T // PARTS, 2048 // PARTS
+    count = [0]
+
+    def next_put(src, dst, peer):
+        count[0] += 1
+        return put(count[0] - 1, src, dst, peer)
+
+    def row_parts(src, first, peer):
+        return [
+            next_put(src.at[pl.ds(R * k, R)], rows.at[pl.ds(first + R * k, R)], peer)
+            for k in range(PARTS)
+        ]
+
+    rows_z = row_parts(grads_in, T, to_z1)
+    rows_y = row_parts(grads_in, 2 * T, to_y)
+    rows_d = row_parts(rows.at[pl.ds(T, T)], 3 * T, to_y)
+    bo_z = [
+        next_put(bo_in.at[x, pl.ds(K * k, K)], bo.at[1, x, pl.ds(K * k, K)], to_z2)
+        for k in range(PARTS)
     ]
+    bo_x = [
+        next_put(bo.at[1, x, pl.ds(K * k, K)], bo.at[1, x, pl.ds(K * k, K)], to_x)
+        for k in range(PARTS)
+    ]
+    acts_z = next_put(acts_in, acts.at[pl.ds(T, T)], to_z1)
+    acts_y = next_put(acts_in, acts.at[pl.ds(2 * T, T)], to_y)
+    acts_d = next_put(acts.at[pl.ds(T, T)], acts.at[pl.ds(3 * T, T)], to_y)
+    ei_z = next_put(ei_in.at[x], ei.at[1, x], to_z2)
+    ei_x = next_put(ei.at[1, x], ei.at[1, x], to_x)
+    bo_c = next_put(bo_in, bo.at[2], to_c)
+    ei_c = next_put(ei_in, ei.at[2], to_c)
+    bo_c1 = next_put(bo.at[1, x], bo.at[3, x], to_c)
+    ei_c1 = next_put(ei.at[1, x], ei.at[3, x], to_c)
+    bo_c2 = next_put(bo.at[1, ox], bo.at[3, ox], to_c)
+    ei_c2 = next_put(ei.at[1, ox], ei.at[3, ox], to_c)
+    pk_z2 = next_put(pk_in.at[x], biq.at[x, 1], to_z2)
+    pk_z1 = next_put(biq.at[x, pl.ds(0, 2)], biq.at[x, pl.ds(2, 2)], to_z1)
+    pk_y = next_put(biq.at[x, pl.ds(0, 4)], biq.at[x, pl.ds(4, 4)], to_y)
+    pk_x = next_put(biq.at[x, pl.ds(0, 8)], biq.at[x, pl.ds(0, 8)], to_x)
+    pk_c1 = next_put(biq.at[x, pl.ds(0, 8)], biq.at[x, pl.ds(8, 8)], to_c)
+    pk_c2 = next_put(biq.at[ox, pl.ds(0, 8)], biq.at[ox, pl.ds(8, 8)], to_c)
+    tok_z = next_put(tok.at[1], got.at[0], to_z1)
+    tok_y = next_put(tok.at[2], got.at[1], to_y)
+    tok_d = next_put(tok.at[3], got.at[2], to_d)
     here = [
         pltpu.make_async_copy(pk_in.at[x], biq.at[x, 0], local.at[0]),
         pltpu.make_async_copy(grads_in, rows.at[pl.ds(0, T)], local.at[1]),
@@ -84,25 +103,13 @@
     pl.semaphore_wait(barrier, 6)
 
     def go(*which):
-        for i in which:
-            cp[i].start()
+        for one in which:
+            one.start()
+            used.append(one)
 
     def came(*which):
-        for i in which:
-            cp[i].wait_recv()
-
-    go(16, 1, 0, 6, 7, 3, 2, 11, 10)
-    here[0].wait()
-    came(16)
-    go(17)
-    came(17)
-    go(18)
-    came(1, 0)
-    go(5, 4)
-    came(18)
-    go(20, 19)
-    for one in here[1:]:
-        one.wait()
+        for one in which:
+            one.wait_recv()
 
     def recips(j):
         for e in range(2):
@@ -112,14 +119,100 @@
                 return 0
             lax.fori_loop(0, 8, step, 0)
 
+    def code_of(slot):
+        at_rows = pl.ds(pl.multiple_of(slot * T, T), T)
+        return at_rows, acts[at_rows, 768:896].astype(jnp.float32)
+
+    def turn_acts(slot, _):
+        at_rows, code = code_of(slot)
+        second = jnp.concatenate([code] * 6, axis=1) >= 4.0
+        both = [
+            lax.dot_general(
+                acts[at_rows, 0:768], bit[e], (((1,), (1,)), ((), ())),
+                preferred_element_type=jnp.float32,
+            )
+            for e in range(2)
+        ]
+        rot_a[at_rows, :] = jnp.where(second, both[1], both[0]).astype(jnp.bfloat16)
+        return 0
+
+    def columns(first, last):
+        def turn_grads(slot, _):
+            at_rows, code = code_of(slot)
+            second = jnp.concatenate([code] * 2, axis=1) >= 4.0
+            both = [
+                jnp.dot(
+                    rows[at_rows, :],
+                    jnp.concatenate([bo[first, e], bo[last, e]], axis=1),
+                    preferred_element_type=jnp.float32,
+                )
+                for e in range(2)
+            ]
+            gt[slot] = jnp.where(second, both[1], both[0]).T.astype(jnp.bfloat16)
+            return 0
+
+        def score(slot, _):
+            at_rows, code = code_of(slot)
+            wide = jnp.concatenate([code] * 6, axis=1)
+            ra = rot_a[at_rows, :].astype(jnp.float32)
+            for doc in range(DOCS_DEV):
+                image = jnp.zeros((2 * T, T), jnp.float32)
+                for e in range(2):
+                    kept = jnp.where(wide == float(4 * e + doc), ra, 0.0).astype(jnp.bfloat16)
+                    summed = jnp.dot(gt[slot], kept, preferred_element_type=jnp.float32)
+                    scale = jnp.concatenate([rc[e, first], rc[e, last]], axis=0)
+                    mat = (summed * scale).astype(jnp.bfloat16)
+                    image = image + jnp.dot(mat, qat[e], preferred_element_type=jnp.float32)
+                part = jnp.sum(image * qgt[...], axis=0, keepdims=True)
+                tok[slot, doc : doc + 1, :] = tok[slot, doc : doc + 1, :] + part
+            return 0
+
+        return turn_grads, score
+
+    def each(lo, hi, step):
+        lax.fori_loop(lo, hi, step, 0)
+
+    go(pk_z2, acts_y, *rows_y, ei_c, bo_c)
+    here[0].wait()
+    came(pk_z2)
+    go(pk_z1, acts_z)
+    for k in range(PARTS):
+        go(rows_z[k], bo_z[k])
+    go(ei_z)
+    for one in here[1:]:
+        one.wait()
+    came(pk_z1)
+    go(pk_y)
+    turn0, score0 = columns(0, 2)
+    turn1, score1 = columns(1, 3)
     recips(0)
-    came(11, 10)
+    came(acts_z)
+    go(acts_d)
+    came(rows_z[0])
+    go(rows_d[0])
+    came(ei_c, bo_c)
+    came(pk_y)
+    go(pk_c1, pk_x)
+    came(bo_z[0])
+    go(bo_x[0])
+    came(rows_z[1])
+    go(rows_d[1])
+    each(0, 1, turn0)
+    for k in range(1, PARTS):
+        came(bo_z[k])
+        go(bo_x[k])
+        if k < PARTS - 1:
+            came(rows_z[k + 1])
+            go(rows_d[k + 1])
+    came(ei_z)
+    go(ei_x, ei_c1, bo_c1)
     recips(2)
-    came(6, 7)
-    go(9, 8, 13, 12)
-    came(19)
-    go(21)
-    came(20, 21)
+    each(1, 2, turn0)
+    came(acts_y, *rows_y)
+    each(2, 3, turn0)
+    came(pk_x)
+    go(pk_c2)
+    came(pk_c1, pk_c2)
 
     for other in range(16):
         oc, oy, oz = other % 2, (other // 2) % 2, other // 4
@@ -149,26 +242,8 @@
     acts[Q : Q + T, 256:896] = quarter[3][:, 0:640]
     ident = quarter[3][:, 640:768].astype(jnp.float32)
 
-    def code_of(slot):
-        at_rows = pl.ds(pl.multiple_of(slot * T, T), T)
-        return at_rows, acts[at_rows, 768:896].astype(jnp.float32)
-
-    came(3, 2, 5, 4)
-
-    def turn_acts(slot, _):
-        at_rows, code = code_of(slot)
-        second = jnp.concatenate([code] * 6, axis=1) >= 4.0
-        each = [
-            lax.dot_general(
-                acts[at_rows, 0:768], bit[e], (((1,), (1,)), ((), ())),
-                preferred_element_type=jnp.float32,
-            )
-            for e in range(2)
-        ]
-        rot_a[at_rows, :] = jnp.where(second, each[1], each[0]).astype(jnp.bfloat16)
-        return 0
-
-    lax.fori_loop(0, 5, turn_acts, 0)
+    each(0, 3, turn_acts)
+    each(4, 5, turn_acts)
     _, qcode = code_of(4)
     qsecond = jnp.concatenate([qcode] * 6, axis=1) >= 4.0
     turned = rot_a[Q : Q + T, :].astype(jnp.float32)
@@ -176,62 +251,34 @@
     qat[1] = jnp.where(qsecond, turned, 0.0).T.astype(jnp.bfloat16)
     tok[...] = jnp.zeros_like(tok)
 
-    def columns(first, last):
-        def turn_grads(slot, _):
-            at_rows, code = code_of(slot)
-            second = jnp.concatenate([code] * 2, axis=1) >= 4.0
-            each = [
-                jnp.dot(
-                    rows[at_rows, :],
-                    jnp.concatenate([bo[first, e], bo[last, e]], axis=1),
-                    preferred_element_type=jnp.float32,
-                )
-                for e in range(2)
-            ]
-            gt[slot] = jnp.where(second, each[1], each[0]).T.astype(jnp.bfloat16)
-            return 0
-
-        lax.fori_loop(0, 5, turn_grads, 0)
-        qgt[...] = gt[4].astype(jnp.float32)
-
-        def score(slot, _):
-            at_rows, code = code_of(slot)
-            wide = jnp.concatenate([code] * 6, axis=1)
-            ra = rot_a[at_rows, :].astype(jnp.float32)
-            for doc in range(DOCS_DEV):
-                image = jnp.zeros((2 * T, T), jnp.float32)
-                for e in range(2):
-                    kept = jnp.where(wide == float(4 * e + doc), ra, 0.0).astype(jnp.bfloat16)
-                    summed = jnp.dot(gt[slot], kept, preferred_element_type=jnp.float32)
-                    scale = jnp.concatenate([rc[e, first], rc[e, last]], axis=0)
-                    mat = (summed * scale).astype(jnp.bfloat16)
-                    image = image + jnp.dot(mat, qat[e], preferred_element_type=jnp.float32)
-                part = jnp.sum(image * qgt[...], axis=0, keepdims=True)
-                tok[slot, doc : doc + 1, :] = tok[slot, doc : doc + 1, :] + part
-            return 0
-
-        lax.fori_loop(0, 4, score, 0)
-
-    columns(0, 2)
-    came(9, 8)
-    go(15, 14)
+    each(4, 5, turn0)
+    qgt[...] = gt[4].astype(jnp.float32)
+    each(0, 3, score0)
+    came(acts_d, *rows_d)
+    each(3, 4, turn_acts)
+    each(3, 4, turn0)
+    came(ei_x, *bo_x)
+    go(ei_c2, bo_c2)
+    each(3, 4, score0)
     recips(1)
-    came(13, 12, 15, 14)
+    came(ei_c1, bo_c1, ei_c2, bo_c2)
     recips(3)
-    columns(1, 3)
-
-    go(22, 23, 24)
+    each(0, 5, turn1)
+    qgt[...] = gt[4].astype(jnp.float32)
+    each(1, 4, score1)
+    go(tok_z, tok_y, tok_d)
+    each(0, 1, score1)
     s_f = lax.broadcasted_iota(jnp.int32, (T, T), 0)
     q_f = lax.broadcasted_iota(jnp.int32, (T, T), 1).astype(jnp.float32)
     owner = ((s_f // 4) * QRY_DEV).astype(jnp.float32)
     table = jnp.where(owner + ident == q_f, 1.0, 0.0)
-    came(22, 23, 24)
+    came(tok_z, tok_y, tok_d)
     total = tok[0] + got[0] + got[1] + got[2]
     res = jnp.dot(
         total, table, precision=lax.Precision.HIGHEST, preferred_element_type=jnp.float32
     )
     out_ref[...] = res[0:4, 0:32]
-    for one in cp:
+    for one in used:
         one.wait_send()
 
 
@@ -274,7 +321,7 @@
             pltpu.SemaphoreType.DMA((LOCALS,)),
         ],
         compiler_params=pltpu.CompilerParams(
-            collective_id=0, has_side_effects=True, vmem_limit_bytes=48 * 2**20
+            collective_id=0, has_side_effects=True, vmem_limit_bytes=60 * 2**20
         ),
     )(train_grads, acts_in, basis_out, eigenvalues, pk_in)
 

time: 115 us -> 95.7 us (0.83)
  Pallas kernels: 108 us -> 90.3 us
  other arithmetic: 4.73 us -> 3.06 us
    pallas_call x1, Pallas kernels: 108 us -> 90.3 us  [fused(): pl.pallas_call(kernel, out_shape=jax.ShapeDtypeStruct((4, 32), f32), in_s...]
where the time goes in v2:
time: 95.7 us; the launch traced here: 95.5 us
  Pallas kernels  90.3 us (94%)
  other arithmetic  3.06 us (3%)
  local copies, waits for them, and re-layouts  2.05 us (2%)
    pallas_call x1, Pallas kernels, fused(): pl.pallas_call(kernel, out_shape=jax.ShapeDtypeStruct((4, 32), f32), in_s...  90.3 us

profile of v2, /device:TPU:0, one launch (start us, length us, event | category | flops | bytes accessed | tf_op | source)
XLA Modules:
  0.0 95.5 jit_solution(4419802538449693601)
XLA Ops:
  0.0 0.7 fusion.3
  0.7 0.1 broadcast_in_dim.26
  0.8 0.0 copy-start.3
  0.8 0.0 copy-start.4
  0.8 0.0 copy-start.1
  0.8 0.0 copy-start
  0.8 1.7 %pad_maximum_fusion.acts_in = bf16[128,896]{1,0:T(8,128)(2,1)} fusion(bf16[128,128]{1,0:T(8,128)(2,1)S(1)} %broadcast_in_dim.26, bf16[128,768]{1,0:T(8,128)(2,1)} %param.11), kind=kLoop, calls=%fused_computation.2 | loop fusion | flops 458752 | bytes 458752 | tf_op jit(solution)/shard_map/concatenate | solution.py:291
  2.5 0.0 copy-done.3
  2.5 0.0 copy-start.2
  2.5 0.1 broadcast_in_dim.28
  2.6 0.0 copy-done.4
  2.6 0.1 broadcast_in_dim.29
  2.6 0.0 copy-done.1
  2.6 0.5 copy-done.2
  3.2 0.0 copy-done
  3.2 0.7 fusion.1.pk_in
  3.9 90.3 %shard_map.109 = f32[4,32]{1,0:T(4,128)} custom-call(bf16[128,2048]{1,0:T(8,128)(2,1)} %grads_in.1, bf16[128,896]{1,0:T(8,128)(2,1)} %pad_maximum_fusion.acts_in, bf16[2,2048,128]{2,1,0:T(8,128)(2,1)} %bo_in.1, bf16[2,128,768]{2,1,0:T(8,128)(2,1)} %ei_in.1, bf16[2,64,768]{2,1,0:T(8,128)(2,1)} %fusion.1.pk_in), custom_call_target="tpu_custom_call" | custom-call | tf_op jit(solution)/shard_map/pallas_call | solution.py:299
  94.3 1.2 %copy.13 = f32[4,32]{1,0:T(4,128)} copy(f32[4,32]{1,0:T(4,128)} %shard_map.109) | data formatting | bytes 1024
  (4 shorter events, 0.0 us)
Async XLA Ops:
  0.8 1.7 %copy-start.3 = (s32[4,1]{0,1:T(1,128)S(1)}, s32[4,1]{0,1:T(1,128)}, u32[]{:S(2)}) copy-start(s32[4,1]{0,1:T(1,128)} %param.17) | copy-start | bytes 52
  0.8 1.8 %copy-start.4 = (s32[4]{0:T(128)S(1)}, s32[4]{0:T(128)}, u32[]{:S(2)}) copy-start(s32[4]{0:T(128)} %param.18) | copy-start | bytes 52
  0.8 1.9 %copy-start.1 = (bf16[4,2048]{1,0:T(4,128)(2,1)S(1)}, bf16[4,2048]{1,0:T(4,128)(2,1)}, u32[]{:S(2)}) copy-start(bf16[4,2048]{1,0:T(4,128)(2,1)} %param.16) | copy-start | bytes 49156
  0.8 2.4 %copy-start = (bf16[2,768,48]{1,2,0:T(8,128)(2,1)S(1)}, bf16[2,768,48]{1,2,0:T(8,128)(2,1)}, u32[]{:S(2)}) copy-start(bf16[2,768,48]{1,2,0:T(8,128)(2,1)} %param.20) | copy-start | bytes 442372
  2.5 0.7 copy-start.2

commit v3 on v2

--- a/solution.py
+++ b/solution.py
@@ -11,7 +11,7 @@
 QCAP = 3
 DAMPING = 0.05
 LANES = 128
-COPIES = 40
+COPIES = 51
 PARTS = 4
 LOCALS = 5
 MESH = pl.DeviceIdType.MESH
@@ -83,9 +83,10 @@
     bo_c2 = next_put(bo.at[1, ox], bo.at[3, ox], to_c)
     ei_c2 = next_put(ei.at[1, ox], ei.at[3, ox], to_c)
     pk_z2 = next_put(pk_in.at[x], biq.at[x, 1], to_z2)
-    pk_z1 = next_put(biq.at[x, pl.ds(0, 2)], biq.at[x, pl.ds(2, 2)], to_z1)
-    pk_y = next_put(biq.at[x, pl.ds(0, 4)], biq.at[x, pl.ds(4, 4)], to_y)
-    pk_x = next_put(biq.at[x, pl.ds(0, 8)], biq.at[x, pl.ds(0, 8)], to_x)
+    own = pk_in.at[x]
+    pk_z1 = [next_put(own if k == 0 else biq.at[x, k], biq.at[x, 2 + k], to_z1) for k in range(2)]
+    pk_y = [next_put(own if k == 0 else biq.at[x, k], biq.at[x, 4 + k], to_y) for k in range(4)]
+    pk_x = [next_put(own if k == 0 else biq.at[x, k], biq.at[x, k], to_x) for k in range(8)]
     pk_c1 = next_put(biq.at[x, pl.ds(0, 8)], biq.at[x, pl.ds(8, 8)], to_c)
     pk_c2 = next_put(biq.at[ox, pl.ds(0, 8)], biq.at[ox, pl.ds(8, 8)], to_c)
     tok_z = next_put(tok.at[1], got.at[0], to_z1)
@@ -172,46 +173,52 @@
     def each(lo, hi, step):
         lax.fori_loop(lo, hi, step, 0)
 
-    go(pk_z2, acts_y, *rows_y, ei_c, bo_c)
+    go(pk_z2, pk_z1[0], pk_y[0], pk_x[0], rows_y[0], rows_z[0], ei_c, bo_c)
+    came(pk_z2)
+    go(pk_z1[1], pk_y[1], pk_x[1], rows_y[1], acts_z, bo_z[0])
+    came(pk_z1[0])
+    go(pk_y[2], pk_x[2], rows_y[2], rows_z[1], bo_z[1])
+    came(pk_z1[1])
+    go(pk_y[3], pk_x[3], rows_y[3], acts_y)
+    go(rows_z[2], bo_z[2], rows_z[3], bo_z[3], ei_z)
+    turn0, score0 = columns(0, 2)
+    turn1, score1 = columns(1, 3)
+    came(pk_y[0])
+    go(pk_x[4])
+    came(rows_z[0], acts_z)
+    go(rows_d[0], acts_d)
+    came(pk_y[1])
+    go(pk_x[5])
+    came(bo_z[0])
+    go(bo_x[0])
+    came(pk_y[2])
+    go(pk_x[6])
+    came(pk_y[3])
     here[0].wait()
-    came(pk_z2)
-    go(pk_z1, acts_z)
-    for k in range(PARTS):
-        go(rows_z[k], bo_z[k])
-    go(ei_z)
+    go(pk_x[7], pk_c1)
+    came(rows_z[1])
+    go(rows_d[1])
+    came(bo_z[1])
+    go(bo_x[1])
     for one in here[1:]:
         one.wait()
-    came(pk_z1)
-    go(pk_y)
-    turn0, score0 = columns(0, 2)
-    turn1, score1 = columns(1, 3)
     recips(0)
-    came(acts_z)
-    go(acts_d)
-    came(rows_z[0])
-    go(rows_d[0])
+    came(rows_z[2])
+    go(rows_d[2])
+    came(bo_z[2])
+    go(bo_x[2])
     came(ei_c, bo_c)
-    came(pk_y)
-    go(pk_c1, pk_x)
-    came(bo_z[0])
-    go(bo_x[0])
-    came(rows_z[1])
-    go(rows_d[1])
     each(0, 1, turn0)
-    for k in range(1, PARTS):
-        came(bo_z[k])
-        go(bo_x[k])
-        if k < PARTS - 1:
-            came(rows_z[k + 1])
-            go(rows_d[k + 1])
-    came(ei_z)
-    go(ei_x, ei_c1, bo_c1)
     recips(2)
+    came(*pk_x)
+    go(pk_c2)
+    came(rows_z[3])
+    go(rows_d[3])
+    came(bo_z[3], ei_z)
+    go(bo_x[3], ei_x, ei_c1, bo_c1)
     each(1, 2, turn0)
     came(acts_y, *rows_y)
     each(2, 3, turn0)
-    came(pk_x)
-    go(pk_c2)
     came(pk_c1, pk_c2)
 
     for other in range(16):

time: 95.7 us -> 82.9 us (0.87)
  Pallas kernels: 90.3 us -> 77.5 us
    pallas_call x1, Pallas kernels: 90.3 us -> 77.5 us  [fused(): pl.pallas_call(kernel, out_shape=jax.ShapeDtypeStruct((4, 32), f32), in_s...]
where the time goes in v3:
time: 82.9 us; the launch traced here: 82.7 us
  Pallas kernels  77.5 us (93%)
  other arithmetic  3.06 us (4%)
  local copies, waits for them, and re-layouts  2.05 us (2%)
    pallas_call x1, Pallas kernels, fused(): pl.pallas_call(kernel, out_shape=jax.ShapeDtypeStruct((4, 32), f32), in_s...  77.5 us
    unnamed x11, local copies, waits for them, and re-layouts  1.8 us
    concatenate x1, other arithmetic, fused(): jnp.concatenate([train_acts, jnp.broadcast_to(code, (LANES, LANES))], axi...  1.66 us

profile of v3, /device:TPU:0, one launch (start us, length us, event | category | flops | bytes accessed | tf_op | source)
XLA Modules:
  0.0 82.7 jit_solution(11922835850642741231)
XLA Ops:
  0.0 0.7 fusion.3
  0.7 0.1 broadcast_in_dim.26
  0.8 0.0 copy-start.3
  0.8 0.0 copy-start.4
  0.8 0.0 copy-start.1
  0.8 0.0 copy-start
  0.8 1.7 %pad_maximum_fusion.acts_in = bf16[128,896]{1,0:T(8,128)(2,1)} fusion(bf16[128,128]{1,0:T(8,128)(2,1)S(1)} %broadcast_in_dim.26, bf16[128,768]{1,0:T(8,128)(2,1)} %param.11), kind=kLoop, calls=%fused_computation.2 | loop fusion | flops 458752 | bytes 458752 | tf_op jit(solution)/shard_map/concatenate | solution.py:298
  2.5 0.0 copy-done.3
  2.5 0.0 copy-start.2
  2.5 0.1 broadcast_in_dim.28
  2.6 0.0 copy-done.4
  2.6 0.1 broadcast_in_dim.29
  2.6 0.0 copy-done.1
  2.6 0.5 copy-done.2
  3.2 0.0 copy-done
  3.2 0.7 fusion.1.pk_in
  3.9 77.5 %shard_map.109 = f32[4,32]{1,0:T(4,128)} custom-call(bf16[128,2048]{1,0:T(8,128)(2,1)} %grads_in.1, bf16[128,896]{1,0:T(8,128)(2,1)} %pad_maximum_fusion.acts_in, bf16[2,2048,128]{2,1,0:T(8,128)(2,1)} %bo_in.1, bf16[2,128,768]{2,1,0:T(8,128)(2,1)} %ei_in.1, bf16[2,64,768]{2,1,0:T(8,128)(2,1)} %fusion.1.pk_in), custom_call_target="tpu_custom_call" | custom-call | tf_op jit(solution)/shard_map/pallas_call | solution.py:306
  81.4 1.2 %copy.13 = f32[4,32]{1,0:T(4,128)} copy(f32[4,32]{1,0:T(4,128)} %shard_map.109) | data formatting | bytes 1024
  (4 shorter events, 0.0 us)
Async XLA Ops:
  0.8 1.7 %copy-start.3 = (s32[4,1]{0,1:T(1,128)S(1)}, s32[4,1]{0,1:T(1,128)}, u32[]{:S(2)}) copy-start(s32[4,1]{0,1:T(1,128)} %param.17) | copy-start | bytes 52
  0.8 1.8 %copy-start.4 = (s32[4]{0:T(128)S(1)}, s32[4]{0:T(128)}, u32[]{:S(2)}) copy-start(s32[4]{0:T(128)} %param.18) | copy-start | bytes 52
  0.8 1.9 %copy-start.1 = (bf16[4,2048]{1,0:T(4,128)(2,1)S(1)}, bf16[4,2048]{1,0:T(4,128)(2,1)}, u32[]{:S(2)}) copy-start(bf16[4,2048]{1,0:T(4,128)(2,1)} %param.16) | copy-start | bytes 49156
  0.8 2.4 %copy-start = (bf16[2,768,48]{1,2,0:T(8,128)(2,1)S(1)}, bf16[2,768,48]{1,2,0:T(8,128)(2,1)}, u32[]{:S(2)}) copy-start(bf16[2,768,48]{1,2,0:T(8,128)(2,1)} %param.20) | copy-start | bytes 442372
  2.5 0.7 copy-start.2

commit v4 on v3

--- a/solution.py
+++ b/solution.py
@@ -175,12 +175,12 @@
 
     go(pk_z2, pk_z1[0], pk_y[0], pk_x[0], rows_y[0], rows_z[0], ei_c, bo_c)
     came(pk_z2)
-    go(pk_z1[1], pk_y[1], pk_x[1], rows_y[1], acts_z, bo_z[0])
+    go(pk_z1[1], pk_y[1], pk_x[1], rows_y[1], acts_z, ei_z, bo_z[0])
     came(pk_z1[0])
     go(pk_y[2], pk_x[2], rows_y[2], rows_z[1], bo_z[1])
     came(pk_z1[1])
     go(pk_y[3], pk_x[3], rows_y[3], acts_y)
-    go(rows_z[2], bo_z[2], rows_z[3], bo_z[3], ei_z)
+    go(rows_z[2], bo_z[2], rows_z[3], bo_z[3])
     turn0, score0 = columns(0, 2)
     turn1, score1 = columns(1, 3)
     came(pk_y[0])
@@ -189,8 +189,8 @@
     go(rows_d[0], acts_d)
     came(pk_y[1])
     go(pk_x[5])
-    came(bo_z[0])
-    go(bo_x[0])
+    came(bo_z[0], ei_z)
+    go(ei_x, bo_x[0])
     came(pk_y[2])
     go(pk_x[6])
     came(pk_y[3])
@@ -210,12 +210,13 @@
     came(ei_c, bo_c)
     each(0, 1, turn0)
     recips(2)
+    go(ei_c1)
     came(*pk_x)
     go(pk_c2)
     came(rows_z[3])
     go(rows_d[3])
-    came(bo_z[3], ei_z)
-    go(bo_x[3], ei_x, ei_c1, bo_c1)
+    came(bo_z[3])
+    go(bo_x[3], bo_c1)
     each(1, 2, turn0)
     came(acts_y, *rows_y)
     each(2, 3, turn0)
@@ -260,16 +261,19 @@
 
     each(4, 5, turn0)
     qgt[...] = gt[4].astype(jnp.float32)
+    came(ei_x)
+    go(ei_c2)
     each(0, 3, score0)
+    recips(1)
+    came(ei_c1, ei_c2)
+    recips(3)
     came(acts_d, *rows_d)
     each(3, 4, turn_acts)
     each(3, 4, turn0)
-    came(ei_x, *bo_x)
-    go(ei_c2, bo_c2)
+    came(*bo_x)
+    go(bo_c2)
     each(3, 4, score0)
-    recips(1)
-    came(ei_c1, bo_c1, ei_c2, bo_c2)
-    recips(3)
+    came(bo_c1, bo_c2)
     each(0, 5, turn1)
     qgt[...] = gt[4].astype(jnp.float32)
     each(1, 4, score1)

time: 82.9 us -> 86.5 us (1.043)
  Pallas kernels: 77.5 us -> 81.1 us
    pallas_call x1, Pallas kernels: 77.5 us -> 81.1 us  [fused(): pl.pallas_call(kernel, out_shape=jax.ShapeDtypeStruct((4, 32), f32), in_s...]
where the time goes in v4:
time: 86.5 us; the launch traced here: 86.3 us
  Pallas kernels  81.1 us (94%)
  other arithmetic  3.06 us (4%)
  local copies, waits for them, and re-layouts  2.05 us (2%)
    pallas_call x1, Pallas kernels, fused(): pl.pallas_call(kernel, out_shape=jax.ShapeDtypeStruct((4, 32), f32), in_s...  81.1 us
    unnamed x11, local copies, waits for them, and re-layouts  1.8 us

profile of v4, /device:TPU:0, one launch (start us, length us, event | category | flops | bytes accessed | tf_op | source)
XLA Modules:
  0.0 86.3 jit_solution(9938029109414887840)
XLA Ops:
  0.0 0.7 fusion.3
  0.7 0.1 broadcast_in_dim.26
  0.8 0.0 copy-start.3
  0.8 0.0 copy-start.4
  0.8 0.0 copy-start.1
  0.8 0.0 copy-start
  0.8 1.7 %pad_maximum_fusion.acts_in = bf16[128,896]{1,0:T(8,128)(2,1)} fusion(bf16[128,128]{1,0:T(8,128)(2,1)S(1)} %broadcast_in_dim.26, bf16[128,768]{1,0:T(8,128)(2,1)} %param.11), kind=kLoop, calls=%fused_computation.2 | loop fusion | flops 458752 | bytes 458752 | tf_op jit(solution)/shard_map/concatenate | solution.py:302
  2.5 0.0 copy-done.3
  2.5 0.0 copy-start.2
  2.5 0.1 broadcast_in_dim.28
  2.6 0.0 copy-done.4
  2.6 0.1 broadcast_in_dim.29
  2.6 0.0 copy-done.1
  2.6 0.5 copy-done.2
  3.2 0.0 copy-done
  3.2 0.7 fusion.1.pk_in
  3.9 81.1 %shard_map.109 = f32[4,32]{1,0:T(4,128)} custom-call(bf16[128,2048]{1,0:T(8,128)(2,1)} %grads_in.1, bf16[128,896]{1,0:T(8,128)(2,1)} %pad_maximum_fusion.acts_in, bf16[2,2048,128]{2,1,0:T(8,128)(2,1)} %bo_in.1, bf16[2,128,768]{2,1,0:T(8,128)(2,1)} %ei_in.1, bf16[2,64,768]{2,1,0:T(8,128)(2,1)} %fusion.1.pk_in), custom_call_target="tpu_custom_call" | custom-call | tf_op jit(solution)/shard_map/pallas_call | solution.py:310
  85.0 1.2 %copy.13 = f32[4,32]{1,0:T(4,128)} copy(f32[4,32]{1,0:T(4,128)} %shard_map.109) | data formatting | bytes 1024
  (4 shorter events, 0.0 us)
Async XLA Ops:
  0.8 1.7 %copy-start.3 = (s32[4,1]{0,1:T(1,128)S(1)}, s32[4,1]{0,1:T(1,128)}, u32[]{:S(2)}) copy-start(s32[4,1]{0,1:T(1,128)} %param.17) | copy-start | bytes 52
  0.8 1.8 %copy-start.4 = (s32[4]{0:T(128)S(1)}, s32[4]{0:T(128)}, u32[]{:S(2)}) copy-start(s32[4]{0:T(128)} %param.18) | copy-start | bytes 52
  0.8 1.9 %copy-start.1 = (bf16[4,2048]{1,0:T(4,128)(2,1)S(1)}, bf16[4,2048]{1,0:T(4,128)(2,1)}, u32[]{:S(2)}) copy-start(bf16[4,2048]{1,0:T(4,128)(2,1)} %param.16) | copy-start | bytes 49156
  0.8 2.4 %copy-start = (bf16[2,768,48]{1,2,0:T(8,128)(2,1)S(1)}, bf16[2,768,48]{1,2,0:T(8,128)(2,1)}, u32[]{:S(2)}) copy-start(bf16[2,768,48]{1,2,0:T(8,128)(2,1)} %param.20) | copy-start | bytes 442372
  2.5 0.7 copy-start.2
